TPU v7x, 256 devices: a whole 4x4x8 slice. The times are simulated.
256 devices in a mesh: dp: 32 (over y_hi, z, core), blk: 8 (over y_lo, x).
Axes of the slice: x: 4, y: 4 (y_hi: 2, y_lo: 2; y = y_hi * 2 + y_lo), z: 8, core: 2. Of those that a mesh axis runs over, the one named last changes fastest.
Arguments:
- tokens: bfloat16 [65536, 2048], P(('dp', 'blk')), may hold values from -24 to 24
- cotangent: bfloat16 [65536, 2048], P(('dp', 'blk')), may hold values from -48 to 48
- slot_token: int32 [57344], P(('dp', 'blk')), may hold values from 0 to 256, as said below
- slot_gate: bfloat16 [57344], P(('dp', 'blk')), may hold values from 0.049804688 to 0.5
- w_gate: bfloat16 [768, 2048], P('blk'), may hold values from -0.125 to 0.125
- w_up: bfloat16 [768, 2048], P('blk'), may hold values from -0.125 to 0.125
- w_down: bfloat16 [768, 2048], P('blk'), may hold values from -0.21875 to 0.21875
Outputs:
- token_grad: bfloat16 [65536, 2048], P(('dp', 'blk'))
- gate_grad: float32 [57344], P(('dp', 'blk'))
- grad_gate: bfloat16 [768, 2048], P('blk', 'dp')
- grad_up: bfloat16 [768, 2048], P('blk', 'dp')
- grad_down: bfloat16 [768, 2048], P('blk', 'dp')
Inputs may be any that keep to these rules, and one draw needn't show every extreme that they name: `slot_token`: on each device its 224 slots name distinct tokens of that same device; the value 256 marks an empty slot, and every device has at least one empty slot.
All inputs are finite; a program needn't handle non-finite values.
Results may differ from a plain program's by a relative error of at most 0.018.
Values may be sent and summed in bfloat16 or wider, within the bound.
A program may use at most 128 MiB of HBM per device.

v0:
```python
import jax
import jax.numpy as jnp
from jax import lax
from jax.sharding import PartitionSpec as P


def shortened(shard):

    def short(part):
        return part.astype(jnp.bfloat16) if part.dtype == jnp.float32 else part

    return jax.tree.map(short, shard)


def passed_along(shard, axis, by):
    size = lax.axis_size(axis)
    return lax.ppermute(shard, axis, [(i, (i + by) % size) for i in range(size)])


def row_dot(left, right):
    return lax.dot_general(
        left, right, (((1,), (1,)), ((), ())), preferred_element_type=jnp.float32
    )


def block_terms(slot_x, slot_dy, gate, w_gate, w_up, w_down):
    weight = gate.astype(jnp.float32)[:, None]
    g = row_dot(slot_x, w_gate)
    u = row_dot(slot_x, w_up)
    sig = jax.nn.sigmoid(g)
    act = g * sig
    hid = act * u
    stored = lax.optimization_barrier(hid.astype(jnp.bfloat16))
    raw = row_dot(slot_dy, w_down)
    gate_part = jnp.sum(stored.astype(jnp.float32) * raw, axis=1)
    grad_h = weight * raw
    grad_g = (grad_h * u * sig * (1.0 + g * (1.0 - sig))).astype(jnp.bfloat16)
    grad_u = (grad_h * act).astype(jnp.bfloat16)
    scaled = (weight * hid).astype(jnp.bfloat16)
    dx_part = jnp.dot(grad_g, w_gate, preferred_element_type=jnp.float32) + jnp.dot(
        grad_u, w_up, preferred_element_type=jnp.float32
    )
    return (dx_part, gate_part, grad_g, grad_u, scaled)


def rotate(weights):
    return jax.tree.map(
        lambda part, own: part.astype(own.dtype),
        passed_along(shortened(weights), "blk", 1),
        weights,
    )


def per_device(tokens, cotangent, slot_token, slot_gate, w_gate, w_up, w_down):
    tok_rows, width = tokens.shape
    slots = slot_token.shape[0]
    hidden_rows = w_gate.shape[0]
    cycle_size = lax.axis_size("blk")
    group_size = lax.axis_size("dp")
    factor = float(tok_rows * cycle_size * group_size) ** (-0.5)
    zero_row = jnp.zeros((1, width), jnp.bfloat16)
    slot_x = jnp.take(jnp.concatenate([tokens, zero_row], axis=0), slot_token, axis=0)
    slot_dy = jnp.take(jnp.concatenate([cotangent, zero_row], axis=0), slot_token, axis=0)
    mine = lax.axis_index("blk")
    weights = (w_gate, w_up, w_down)
    dx_slot = jnp.zeros((slots, width), jnp.float32)
    gate_sum = jnp.zeros((slots,), jnp.float32)
    cols = width // group_size
    split_x = slot_x.reshape(slots, group_size, cols)
    split_dy = slot_dy.reshape(slots, group_size, cols)
    partial_value = jnp.zeros((group_size, cycle_size, 3, hidden_rows, cols), jnp.float32)
    for step in range(cycle_size):
        dx_part, gate_part, grad_g, grad_u, scaled = block_terms(
            slot_x, slot_dy, slot_gate, weights[0], weights[1], weights[2]
        )
        dx_slot = dx_slot + dx_part
        gate_sum = gate_sum + gate_part
        block = jnp.stack(
            [
                jnp.einsum("sh,spe->phe", grad_g, split_x, preferred_element_type=jnp.float32),
                jnp.einsum("sh,spe->phe", grad_u, split_x, preferred_element_type=jnp.float32),
                jnp.einsum("sh,spe->phe", scaled, split_dy, preferred_element_type=jnp.float32),
            ],
            axis=1,
        )
        owner = (mine - step) % cycle_size
        partial_value = lax.dynamic_update_slice_in_dim(partial_value, block[:, None], owner, 1)
        if step + 1 < cycle_size:
            weights = rotate(weights)
    terms = partial_value.reshape(group_size * cycle_size, 3, hidden_rows, cols)
    summed = lax.psum_scatter(terms, ("dp", "blk"), scatter_dimension=0, tiled=True)[0]
    token_grad = (
        jnp.zeros((tok_rows + 1, width), jnp.float32)
        .at[slot_token]
        .add(dx_slot)[:tok_rows]
        .astype(jnp.bfloat16)
    )
    summed = summed * factor
    return (
        token_grad,
        gate_sum,
        summed[0].astype(jnp.bfloat16),
        summed[1].astype(jnp.bfloat16),
        summed[2].astype(jnp.bfloat16),
    )


def solution(mesh):
    in_specs = (
        P(("dp", "blk"), None),
        P(("dp", "blk"), None),
        P(("dp", "blk")),
        P(("dp", "blk")),
        P("blk", None),
        P("blk", None),
        P("blk", None),
    )
    out_specs = (
        P(("dp", "blk"), None),
        P(("dp", "blk")),
        P("blk", "dp"),
        P("blk", "dp"),
        P("blk", "dp"),
    )
    return jax.shard_map(
        per_device, mesh=mesh, in_specs=in_specs, out_specs=out_specs, check_vma=False
    )
```

profile of v0, /device:TPU:1, one launch (start us, length us, event | category | flops | bytes accessed | tf_op | source)
XLA Modules:
  0.0 1531.3 jit_solution(16358683041494642837)
XLA Ops:
  15.5 2.2 gather_fusion
  17.7 2.2 gather_fusion.1
  24.5 2.8 convolution_bitcast_fusion.21
  30.0 5.3 collective-permute-done.2
  44.5 7.7 collective-permute-done.5
  53.8 6.8 collective-permute-done.3
  63.0 6.0 collective-permute-done.7
  69.8 7.7 collective-permute-done.8
  79.1 6.8 collective-permute-done.6
  89.1 5.2 collective-permute-done.10
  95.1 7.7 collective-permute-done.11
  104.4 6.8 collective-permute-done.9
  114.4 5.2 collective-permute-done.13
  120.3 7.7 collective-permute-done.14
  129.7 6.8 collective-permute-done.12
  139.9 5.1 collective-permute-done.16
  146.4 15.4 %collective-permute-done.15 = bf16[96,2048]{1,0:T(8,128)(2,1)} collective-permute-done((bf16[96,2048]{1,0:T(8,128)(2,1)S(1)}, bf16[96,2048]{1,0:T(8,128)(2,1)}, u32[]{:S(2)}, u32[]{:S(2)}) %collective-permute-start.15) | collective-permute-done | bytes 393248 | tf_op jit(solution)/shard_map/ppermute | solution.py:17
  174.3 11.6 broadcast_in_dim.53
  185.9 4.1 copy_dynamic-update-slice_fusion.7
  193.5 2.7 collective-permute-done.20
  196.3 2.4 multiply_convert_fusion.10
  233.4 2.6 fusion
  236.1 4.9 scatter_custom_fusion
  242.9 1279.5 %reduce-scatter.2.cloned.1.call-done = f32[1,3,96,64]{2,3,1,0:T(8,128)} async-done(((f32[256,3,96,64]{2,3,1,0:T(8,128)}), f32[1,3,96,64]{2,3,1,0:T(8,128)}) %reduce-scatter.2.cloned.1.call-update) | async-done | bytes 73744 | tf_op jit(solution)/shard_map/reduce_scatter | solution.py:91
  (312 shorter events, 100.2 us)
Async XLA Ops:
  7.2 1515.3 %reduce-scatter.2.cloned.1.call-start = ((), (), s32[]{:S(2)}) async-start(), calls=%async_computation.1 | async-start | bytes 25264128 | tf_op jit(solution)/shard_map/reduce_scatter | solution.py:91
  7.2 21.5 %collective-permute-start.1 = (bf16[96,2048]{1,0:T(8,128)(2,1)}, bf16[96,2048]{1,0:T(8,128)(2,1)}, u32[]{:S(2)}, u32[]{:S(2)}) collective-permute-start(bf16[96,2048]{1,0:T(8,128)(2,1)} %param.14), channel_id=1, source_target_pairs={{0,1},{1,2},{2,3},{3,4},{4,5},{5,6},{6,7},{7,0},{8,9},{9,10},{10,1... | collective-permute-start | bytes 1179656 | tf_op jit(solution)/shard_map/ppermute | solution.py:17
  9.3 28.6 %collective-permute-start = (bf16[96,2048]{1,0:T(8,128)(2,1)}, bf16[96,2048]{1,0:T(8,128)(2,1)}, u32[]{:S(2)}, u32[]{:S(2)}) collective-permute-start(bf16[96,2048]{1,0:T(8,128)(2,1)} %param.15), channel_id=1, source_target_pairs={{0,1},{1,2},{2,3},{3,4},{4,5},{5,6},{6,7},{7,0},{8,9},{9,10},{10,1... | collective-permute-start | bytes 1179656 | tf_op jit(solution)/shard_map/ppermute | solution.py:17
  10.5 24.8 %collective-permute-start.2 = (bf16[96,2048]{1,0:T(8,128)(2,1)}, bf16[96,2048]{1,0:T(8,128)(2,1)S(1)}, u32[]{:S(2)}, u32[]{:S(2)}) collective-permute-start(bf16[96,2048]{1,0:T(8,128)(2,1)} %param.13), channel_id=1, source_target_pairs={{0,1},{1,2},{2,3},{3,4},{4,5},{5,6},{6,7},{7,0},{8,9},{9,10},{10,1... | collective-permute-start | bytes 1179656 | tf_op jit(solution)/shard_map/ppermute | solution.py:17
  28.7 134.6 %copy-start.50 = (f32[224,96]{0,1:T(8,128)}, f32[224,96]{0,1:T(8,128)S(1)}, u32[]{:S(2)}) copy-start(f32[224,96]{0,1:T(8,128)S(1)} %fusion.73) | copy-start | bytes 258052
  28.7 15.0 collective-permute-start.4
  35.3 16.9 %collective-permute-start.5 = (bf16[96,2048]{1,0:T(8,128)(2,1)S(1)}, bf16[96,2048]{1,0:T(8,128)(2,1)S(1)}, u32[]{:S(2)}, u32[]{:S(2)}) collective-permute-start(bf16[96,2048]{1,0:T(8,128)(2,1)S(1)} %collective-permute-done.2), channel_id=1, source_target_pairs={{0,1},{1,2},{2,3},{3,4},{4,5},{5,6},{6,7},{7,0},{8,9},{9,10},{10,1... | collective-permute-start | bytes 1179656 | tf_op jit(solution)/shard_map/ppermute | solution.py:17
  38.0 22.6 %collective-permute-start.3 = (bf16[96,2048]{1,0:T(8,128)(2,1)}, bf16[96,2048]{1,0:T(8,128)(2,1)S(1)}, u32[]{:S(2)}, u32[]{:S(2)}) collective-permute-start(bf16[96,2048]{1,0:T(8,128)(2,1)} %collective-permute-done), channel_id=1, source_target_pairs={{0,1},{1,2},{2,3},{3,4},{4,5},{5,6},{6,7},{7,0},{8,9},{9,10},{10,1... | collective-permute-start | bytes 1179656 | tf_op jit(solution)/shard_map/ppermute | solution.py:17
  43.8 25.3 %collective-permute-start.7 = (bf16[96,2048]{1,0:T(8,128)(2,1)S(1)}, bf16[96,2048]{1,0:T(8,128)(2,1)S(1)}, u32[]{:S(2)}, u32[]{:S(2)}) collective-permute-start(bf16[96,2048]{1,0:T(8,128)(2,1)S(1)} %collective-permute-done.4), channel_id=1, source_target_pairs={{0,1},{1,2},{2,3},{3,4},{4,5},{5,6},{6,7},{7,0},{8,9},{9,10},{10,1... | collective-permute-start | bytes 1179656 | tf_op jit(solution)/shard_map/ppermute | solution.py:17
  52.2 25.3 %collective-permute-start.8 = (bf16[96,2048]{1,0:T(8,128)(2,1)S(1)}, bf16[96,2048]{1,0:T(8,128)(2,1)S(1)}, u32[]{:S(2)}, u32[]{:S(2)}) collective-permute-start(bf16[96,2048]{1,0:T(8,128)(2,1)S(1)} %collective-permute-done.5), channel_id=1, source_target_pairs={{0,1},{1,2},{2,3},{3,4},{4,5},{5,6},{6,7},{7,0},{8,9},{9,10},{10,1... | collective-permute-start | bytes 1179656 | tf_op jit(solution)/shard_map/ppermute | solution.py:17
  60.6 25.3 %collective-permute-start.6 = (bf16[96,2048]{1,0:T(8,128)(2,1)S(1)}, bf16[96,2048]{1,0:T(8,128)(2,1)S(1)}, u32[]{:S(2)}, u32[]{:S(2)}) collective-permute-start(bf16[96,2048]{1,0:T(8,128)(2,1)S(1)} %collective-permute-done.3), channel_id=1, source_target_pairs={{0,1},{1,2},{2,3},{3,4},{4,5},{5,6},{6,7},{7,0},{8,9},{9,10},{10,1... | collective-permute-start | bytes 1179656 | tf_op jit(solution)/shard_map/ppermute | solution.py:17
  69.0 25.3 %collective-permute-start.10 = (bf16[96,2048]{1,0:T(8,128)(2,1)S(1)}, bf16[96,2048]{1,0:T(8,128)(2,1)S(1)}, u32[]{:S(2)}, u32[]{:S(2)}) collective-permute-start(bf16[96,2048]{1,0:T(8,128)(2,1)S(1)} %collective-permute-done.7), channel_id=1, source_target_pairs={{0,1},{1,2},{2,3},{3,4},{4,5},{5,6},{6,7},{7,0},{8,9},{9,10},{10,1... | collective-permute-start | bytes 1179656 | tf_op jit(solution)/shard_map/ppermute | solution.py:17
  77.5 25.3 %collective-permute-start.11 = (bf16[96,2048]{1,0:T(8,128)(2,1)S(1)}, bf16[96,2048]{1,0:T(8,128)(2,1)S(1)}, u32[]{:S(2)}, u32[]{:S(2)}) collective-permute-start(bf16[96,2048]{1,0:T(8,128)(2,1)S(1)} %collective-permute-done.8), channel_id=1, source_target_pairs={{0,1},{1,2},{2,3},{3,4},{4,5},{5,6},{6,7},{7,0},{8,9},{9,10},{10,1... | collective-permute-start | bytes 1179656 | tf_op jit(solution)/shard_map/ppermute | solution.py:17
  85.9 25.3 %collective-permute-start.9 = (bf16[96,2048]{1,0:T(8,128)(2,1)S(1)}, bf16[96,2048]{1,0:T(8,128)(2,1)S(1)}, u32[]{:S(2)}, u32[]{:S(2)}) collective-permute-start(bf16[96,2048]{1,0:T(8,128)(2,1)S(1)} %collective-permute-done.6), channel_id=1, source_target_pairs={{0,1},{1,2},{2,3},{3,4},{4,5},{5,6},{6,7},{7,0},{8,9},{9,10},{10,1... | collective-permute-start | bytes 1179656 | tf_op jit(solution)/shard_map/ppermute | solution.py:17
  94.3 25.3 %collective-permute-start.13 = (bf16[96,2048]{1,0:T(8,128)(2,1)S(1)}, bf16[96,2048]{1,0:T(8,128)(2,1)S(1)}, u32[]{:S(2)}, u32[]{:S(2)}) collective-permute-start(bf16[96,2048]{1,0:T(8,128)(2,1)S(1)} %collective-permute-done.10), channel_id=1, source_target_pairs={{0,1},{1,2},{2,3},{3,4},{4,5},{5,6},{6,7},{7,0},{8,9},{9,10},{10,1... | collective-permute-start | bytes 1179656 | tf_op jit(solution)/shard_map/ppermute | solution.py:17
  102.7 25.3 %collective-permute-start.14 = (bf16[96,2048]{1,0:T(8,128)(2,1)S(1)}, bf16[96,2048]{1,0:T(8,128)(2,1)S(1)}, u32[]{:S(2)}, u32[]{:S(2)}) collective-permute-start(bf16[96,2048]{1,0:T(8,128)(2,1)S(1)} %collective-permute-done.11), channel_id=1, source_target_pairs={{0,1},{1,2},{2,3},{3,4},{4,5},{5,6},{6,7},{7,0},{8,9},{9,10},{10,1... | collective-permute-start | bytes 1179656 | tf_op jit(solution)/shard_map/ppermute | solution.py:17
  111.2 25.3 %collective-permute-start.12 = (bf16[96,2048]{1,0:T(8,128)(2,1)S(1)}, bf16[96,2048]{1,0:T(8,128)(2,1)S(1)}, u32[]{:S(2)}, u32[]{:S(2)}) collective-permute-start(bf16[96,2048]{1,0:T(8,128)(2,1)S(1)} %collective-permute-done.9), channel_id=1, source_target_pairs={{0,1},{1,2},{2,3},{3,4},{4,5},{5,6},{6,7},{7,0},{8,9},{9,10},{10,1... | collective-permute-start | bytes 1179656 | tf_op jit(solution)/shard_map/ppermute | solution.py:17
  119.6 25.4 %collective-permute-start.16 = (bf16[96,2048]{1,0:T(8,128)(2,1)S(1)}, bf16[96,2048]{1,0:T(8,128)(2,1)}, u32[]{:S(2)}, u32[]{:S(2)}) collective-permute-start(bf16[96,2048]{1,0:T(8,128)(2,1)S(1)} %collective-permute-done.13), channel_id=1, source_target_pairs={{0,1},{1,2},{2,3},{3,4},{4,5},{5,6},{6,7},{7,0},{8,9},{9,10},{10,1... | collective-permute-start | bytes 1179656 | tf_op jit(solution)/shard_map/ppermute | solution.py:17
  128.0 35.3 %collective-permute-start.17 = (bf16[96,2048]{1,0:T(8,128)(2,1)S(1)}, bf16[96,2048]{1,0:T(8,128)(2,1)}, u32[]{:S(2)}, u32[]{:S(2)}) collective-permute-start(bf16[96,2048]{1,0:T(8,128)(2,1)S(1)} %collective-permute-done.14), channel_id=1, source_target_pairs={{0,1},{1,2},{2,3},{3,4},{4,5},{5,6},{6,7},{7,0},{8,9},{9,10},{10,1... | collective-permute-start | bytes 1179656 | tf_op jit(solution)/shard_map/ppermute | solution.py:17
  129.7 33.6 %copy-start.44 = (f32[224,96]{0,1:T(8,128)}, f32[224,96]{0,1:T(8,128)S(1)}, u32[]{:S(2)}) copy-start(f32[224,96]{0,1:T(8,128)S(1)} %fusion.95) | copy-start | bytes 258052
  136.5 25.4 %collective-permute-start.15 = (bf16[96,2048]{1,0:T(8,128)(2,1)S(1)}, bf16[96,2048]{1,0:T(8,128)(2,1)}, u32[]{:S(2)}, u32[]{:S(2)}) collective-permute-start(bf16[96,2048]{1,0:T(8,128)(2,1)S(1)} %collective-permute-done.12), channel_id=1, source_target_pairs={{0,1},{1,2},{2,3},{3,4},{4,5},{5,6},{6,7},{7,0},{8,9},{9,10},{10,1... | collective-permute-start | bytes 1179656 | tf_op jit(solution)/shard_map/ppermute | solution.py:17
  169.7 20.9 %collective-permute-start.19 = (bf16[96,2048]{1,0:T(8,128)(2,1)}, bf16[96,2048]{1,0:T(8,128)(2,1)}, u32[]{:S(2)}, u32[]{:S(2)}) collective-permute-start(bf16[96,2048]{1,0:T(8,128)(2,1)} %collective-permute-done.16), channel_id=1, source_target_pairs={{0,1},{1,2},{2,3},{3,4},{4,5},{5,6},{6,7},{7,0},{8,9},{9,10},{10,1... | collective-permute-start | bytes 1179656 | tf_op jit(solution)/shard_map/ppermute | solution.py:17
  171.9 20.1 %collective-permute-start.18 = (bf16[96,2048]{1,0:T(8,128)(2,1)}, bf16[96,2048]{1,0:T(8,128)(2,1)}, u32[]{:S(2)}, u32[]{:S(2)}) collective-permute-start(bf16[96,2048]{1,0:T(8,128)(2,1)} %collective-permute-done.15), channel_id=1, source_target_pairs={{0,1},{1,2},{2,3},{3,4},{4,5},{5,6},{6,7},{7,0},{8,9},{9,10},{10,1... | collective-permute-start | bytes 1179656 | tf_op jit(solution)/shard_map/ppermute | solution.py:17
  173.4 22.8 %collective-permute-start.20 = (bf16[96,2048]{1,0:T(8,128)(2,1)}, bf16[96,2048]{1,0:T(8,128)(2,1)}, u32[]{:S(2)}, u32[]{:S(2)}) collective-permute-start(bf16[96,2048]{1,0:T(8,128)(2,1)} %collective-permute-done.17), channel_id=1, source_target_pairs={{0,1},{1,2},{2,3},{3,4},{4,5},{5,6},{6,7},{7,0},{8,9},{9,10},{10,1... | collective-permute-start | bytes 1179656 | tf_op jit(solution)/shard_map/ppermute | solution.py:17
  (97 other events, 595.1 us)
Sparse Core Ops, SparseCore 0:
  219.1 1303.2 reduce-scatter.1
where the time goes:
time: 1550 us; the launch traced here: 1530 us
  waiting for transfers between devices  1380 us (89%)
  matrix products  56.8 us (4%)
  other arithmetic  28 us (2%)
  local copies, waits for them, and re-layouts  26.1 us (2%)
  starting transfers between devices  20.4 us (1%)
  between operations  16.1 us (1%)
    reduce_scatter x1, waiting for transfers between devices, per_device(): lax.psum_scatter(terms, ('dp', 'blk'), scatter_dimension=0, tiled=True)[0]  1280 us
    ppermute x21, waiting for transfers between devices, passed_along(): lax.ppermute(shard, axis, [(i, (i + by) % size) for i in range(size)])  104 us
  transfers between devices with their start and end apart: 22, of which 17 were waited for; matrix products, arithmetic and copies ran while one was open for 5% of the time, Pallas kernels for 0%

commit v1 on v0

v1 whole, which is shorter than its diff:
```python
import jax
import jax.numpy as jnp
from jax import lax
from jax.experimental import pallas as pl
from jax.experimental.pallas import tpu as pltpu
from jax.sharding import PartitionSpec as P

MESH = pl.DeviceIdType.MESH
F32 = jnp.float32
BF16 = jnp.bfloat16
TICKS = 4
UNIT = 48


def dot_nt(a, b):
    return lax.dot_general(a, b, (((1,), (1,)), ((), ())), preferred_element_type=F32)


def dot_nn(a, b):
    return lax.dot_general(a, b, (((1,), (0,)), ((), ())), preferred_element_type=F32)


def kernel(
    factor, tok, cot, slot, gate, wg, wu, wd,
    out_x, out_gate, out_g, out_u, out_d,
    xb, db, cb, ups, raws, wgu, wdn, dgs, grad, recv, fin, pack, a2, dxo, dxs, dxr, gs, gr,
    loc_sem, sib_s, sib_r, ax_s, ay_s, ag_r, zs, zr, ps, pr,
):
    dp, blk = lax.axis_index("dp"), lax.axis_index("blk")
    c, z, yh = dp % 2, (dp // 2) % 8, dp // 16
    x, yl = blk % 4, blk // 4
    y = yh * 2 + yl
    home = c == yl
    away = c != yl

    def device(xx, yy, zz, cc):
        return ((yy // 2) * 16 + zz * 2 + cc, (yy % 2) * 4 + xx)

    right, left = device((x + 1) % 4, y, z, c), device((x + 3) % 4, y, z, c)
    above, below = device(x, (y + 1) % 4, z, c), device(x, (y + 3) % 4, z, c)
    zside = (device(x, y, (z + 1) % 8, c), device(x, y, (z + 7) % 8, c))
    sibling = device(x, y, z, 1 - c)
    place = y * 4 + x

    loads = [
        pltpu.make_async_copy(tok, xb.at[pl.ds(0, 256)], loc_sem.at[0]),
        pltpu.make_async_copy(cot, db.at[pl.ds(0, 256)], loc_sem.at[1]),
    ]
    wloads = [
        pltpu.make_async_copy(wg.at[pl.ds(0, 48)], wgu.at[pl.ds(0, 48)], loc_sem.at[2]),
        pltpu.make_async_copy(wu.at[pl.ds(0, 48)], wgu.at[pl.ds(48, 48)], loc_sem.at[3]),
        pltpu.make_async_copy(wg.at[pl.ds(48, 48)], wgu.at[pl.ds(96, 48)], loc_sem.at[4]),
        pltpu.make_async_copy(wu.at[pl.ds(48, 48)], wgu.at[pl.ds(144, 48)], loc_sem.at[5]),
        pltpu.make_async_copy(wd, wdn.at[pl.ds(0, 96)], loc_sem.at[6]),
    ]

    @pl.when(home)
    def _():
        for copy in wloads:
            copy.start()

    for copy in loads:
        copy.start()

    barrier = pltpu.get_barrier_semaphore()

    def greet(target):
        pl.semaphore_signal(barrier, inc=1, device_id=target, device_id_type=MESH)

    greet(zside[0])
    greet(zside[1])
    greet(sibling)

    def greet_plane(r, carry):
        other = (place + r) % 16
        greet(device(other % 4, other // 4, z, yl))
        return carry

    lax.fori_loop(1, 16, greet_plane, 0)

    @pl.when(away)
    def _():
        greet(above)
        greet(below)

    slots = jnp.broadcast_to(slot[...].astype(F32), (128, 224)).T[:, 0:1]
    gates = jnp.broadcast_to(gate[...].astype(F32), (128, 224)).T[:, 0:1]
    token_of = lax.broadcasted_iota(jnp.int32, (224, 256), 1).astype(F32)
    named = token_of == slots
    cb[0] = jnp.broadcast_to(
        jnp.sum(jnp.where(named, gates, 0.0), axis=0, keepdims=True), (8, 256)
    )

    @pl.when(home)
    def _():
        for copy in wloads:
            copy.wait()

    for copy in loads:
        copy.wait()
    pl.semaphore_wait(barrier, 19)

    def remote(src, dst, s_sem, r_sem, target):
        return pltpu.make_async_remote_copy(
            src_ref=src, dst_ref=dst, send_sem=s_sem, recv_sem=r_sem,
            device_id=target, device_id_type=MESH,
        )

    def unit(t, i):
        return (wgu.at[pl.ds(192 * t + 96 * i, 96)], wdn.at[pl.ds(96 * t + 48 * i, 48)])

    def send_unit(src, dst, sem, n, target):
        a, b = unit(*src), unit(*dst)
        return [
            remote(a[p], b[p], sem.at[n, p], ag_r.at[dst[0], dst[1], p], target)
            for p in range(2)
        ]

    def ring_a():
        return send_unit((0, 0), (1, 0), ax_s, 0, right) + send_unit((0, 0), (1, 1), ax_s, 1, left)

    def ring_b():
        return send_unit((0, 1), (2, 0), ax_s, 2, right) + send_unit((0, 1), (2, 1), ax_s, 3, left)

    def ring_f(t):
        if t == 1:
            return send_unit((1, 0), (3, 0), ax_s, 4, right)
        return send_unit((2, 1), (3, 1), ax_s, 5, left)

    def up_down(t):
        return send_unit((t, 0), (t, 0), ay_s, 2 * t, below) + send_unit((t, 1), (t, 1), ay_s, 2 * t + 1, above)

    def start(copies):
        for copy in copies:
            copy.start()

    def wait_unit(t, i):
        for p in range(2):
            ref = unit(t, i)[p]
            remote(ref, ref, ax_s.at[0, p], ag_r.at[t, i, p], sibling).wait_recv()

    sib = [
        remote(xb.at[pl.ds(0, 256)], xb.at[pl.ds(256, 256)], sib_s.at[0], sib_r.at[0], sibling),
        remote(db.at[pl.ds(0, 256)], db.at[pl.ds(256, 256)], sib_s.at[1], sib_r.at[1], sibling),
        remote(cb.at[0], cb.at[1], sib_s.at[2], sib_r.at[2], sibling),
    ]

    @pl.when(home)
    def _():
        start(ring_a() + up_down(0))

    start(sib)

    gate_acc = [jnp.zeros((1, 512), F32)]

    def compute(t):
        top, low = 192 * t, 96 * t

        def forward(n, carry):
            rows = pl.ds(pl.multiple_of(n * 256, 256), 256)
            ups[n] = dot_nt(wgu[pl.ds(top, 192)], xb[rows])
            return carry

        def outer(n, carry):
            rows = pl.ds(pl.multiple_of(n * 256, 256), 256)
            raws[n] = dot_nt(wdn[pl.ds(low, 96)], db[rows])
            return carry

        lax.fori_loop(0, 2, forward, 0)
        lax.fori_loop(0, 2, outer, 0)
        gu = jnp.concatenate([ups[0], ups[1]], axis=1)
        raw2 = jnp.concatenate([raws[0], raws[1]], axis=1)
        weight = jnp.concatenate([cb[0, 0:1], cb[1, 0:1]], axis=1)
        scaled = []
        for i in range(2):
            g = gu[96 * i : 96 * i + 48]
            u = gu[96 * i + 48 : 96 * i + 96]
            raw = raw2[48 * i : 48 * i + 48]
            sig = 1.0 / (1.0 + jnp.exp(-g))
            act = g * sig
            hid = act * u
            stored = hid.astype(BF16).astype(F32)
            gate_acc[0] = gate_acc[0] + jnp.sum(stored * raw, axis=0, keepdims=True)
            dh = weight * raw
            dgs[pl.ds(top + 96 * i, 48)] = (dh * u * sig * (1.0 + g * (1.0 - sig))).astype(BF16)
            dgs[pl.ds(top + 96 * i + 48, 48)] = (dh * act).astype(BF16)
            scaled.append((weight * hid).astype(BF16))
        q = jnp.concatenate(scaled, axis=0)
        dgu = dgs[pl.ds(top, 192)]

        def columns(n, carry):
            cols = pl.ds(pl.multiple_of(n * 256, 256), 256)
            part = dot_nn(dgu, xb[:, cols]).astype(BF16)
            for k in range(2):
                grad[t, 2 * (n % 4) + k, n // 4, 0:192] = part[:, 128 * k : 128 * k + 128]
            return carry

        def columns_down(n, carry):
            cols = pl.ds(pl.multiple_of(n * 256, 256), 256)
            down = dot_nn(q, db[:, cols]).astype(BF16)
            for k in range(2):
                grad[t, 2 * (n % 4) + k, n // 4, 192:288] = down[:, 128 * k : 128 * k + 128]
            return carry

        lax.fori_loop(0, 8, columns_down, 0)
        lax.fori_loop(0, 8, columns, 0)

    def ring(t, way, step):
        sign = 1 if way == 0 else 7
        dest = (z + sign * (5 - step)) % 8
        if step == 1:
            src, dst = grad.at[t, dest, way], recv.at[t, way, 0, way]
        else:
            src, dst = grad.at[t, dest], recv.at[t, way, step - 1]
        return remote(src, dst, zs.at[t, way, step - 1], zr.at[t, way, step - 1], zside[way])

    def first(t):
        for way in range(2):
            ring(t, way, 1).start()

    def pass_on(t, step):
        for way in range(2):
            ring(t, way, step - 1).wait_recv()
            sign = 1 if way == 0 else 7
            dest = (z + sign * (5 - step)) % 8
            for h in (way,) if step == 2 else (0, 1):
                total = grad[t, dest, h].astype(F32) + recv[t, way, step - 2, h].astype(F32)
                grad[t, dest, h] = total.astype(BF16)
            ring(t, way, step).start()

    def finish(t):
        for way in range(2):
            ring(t, way, 4).wait_recv()
        for h in range(2):
            fin[t, h] = (
                grad[t, z, h].astype(F32) + recv[t, 0, 3, h].astype(F32) + recv[t, 1, 3, h].astype(F32)
            )

    low_lanes = lax.broadcasted_iota(jnp.int32, (144, 128), 1) < 64
    halves = (((0, 0), (0, 1)), ((1, 0), (2, 0)), ((1, 1), (2, 1)), ((3, 0), (3, 1)))
    offset = (0, 3, 1, 2)

    def rows_of(t, i, h):
        return jnp.concatenate(
            [fin[t, h, pl.ds(96 * i, 96)], fin[t, h, pl.ds(192 + 48 * i, 48)]], axis=0
        )

    def deliver_copy(j, yy, kk):
        h, k = (yh + yy) % 2, (c + kk) % 2
        target = device((x + offset[j]) % 4, 2 * h + c, z, k)
        return remote(pack.at[j, h, k], a2.at[place], ps.at[j, yy, kk], pr.at[place], target)

    def deliver(j):
        for h in range(2):
            a, b = rows_of(*halves[j][0], h), rows_of(*halves[j][1], h)
            pack[j, h, 0] = jnp.where(low_lanes, a, pltpu.roll(b, 64, 1)).astype(BF16)
            pack[j, h, 1] = jnp.where(low_lanes, pltpu.roll(a, 64, 1), b).astype(BF16)
        for yy in range(2):
            for kk in range(2):
                if (j, yy, kk) == (0, 0, 0):

                    @pl.when(away)
                    def _():
                        deliver_copy(0, 0, 0).start()

                    @pl.when(home)
                    def _():
                        a2[place] = pack[0, yh, c]

                else:
                    deliver_copy(j, yy, kk).start()

    dx_copy = remote(dxs, dxr, sib_s.at[3], sib_r.at[3], sibling)
    gate_copy = remote(gs, gr, sib_s.at[4], sib_r.at[4], sibling)

    def token_part():
        gs[...] = jnp.broadcast_to(gate_acc[0][:, 256:], (8, 256))
        gate_copy.start()
        left_side = dgs[...].T

        def columns(n, carry):
            cols = pl.ds(pl.multiple_of(n * 256, 256), 256)
            part = dot_nn(left_side, wgu[:, cols])
            dxo[:, cols] = part[:256]
            dxs[:, cols] = part[256:]
            return carry

        lax.fori_loop(0, 8, columns, 0)
        dx_copy.start()

    def weights_of(t):
        @pl.when(away)
        def _():
            wait_unit(t, 0)
            wait_unit(t, 1)

        if t > 0:

            @pl.when(home)
            def _():
                wait_unit(t, 0)
                wait_unit(t, 1)
                if t < 3:
                    start(ring_f(t))
                start(up_down(t))

    for copy in sib:
        copy.wait_recv()
    weights_of(0)
    compute(0)
    first(0)

    @pl.when(home)
    def _():
        start(ring_b())

    pass_on(0, 2)
    weights_of(1)
    compute(1)
    first(1)
    pass_on(0, 3)
    pass_on(1, 2)
    pass_on(0, 4)
    weights_of(2)
    compute(2)
    first(2)
    finish(0)
    deliver(0)
    pass_on(1, 3)
    pass_on(2, 2)
    pass_on(1, 4)
    weights_of(3)
    compute(3)
    first(3)
    finish(1)
    pass_on(2, 3)
    pass_on(3, 2)
    token_part()
    pass_on(2, 4)
    pass_on(3, 3)
    finish(2)
    deliver(1)
    deliver(2)
    pass_on(3, 4)

    gate_copy.wait_recv()
    gate_tok = gate_acc[0][:, :256] + gr[0:1]
    column = jnp.sum(jnp.where(named, gate_tok, 0.0), axis=1, keepdims=True)
    out_gate[...] = jnp.broadcast_to(column, (224, 128)).T[0:1]
    dx_copy.wait_recv()
    out_x[...] = (dxo[...] + dxr[...]).astype(BF16)

    finish(3)
    deliver(3)

    @pl.when(away)
    def _():
        remote(a2.at[place], a2.at[place], ps.at[0, 0, 0], pr.at[place], sibling).wait_recv()

    def arrival(r, carry):
        other = (place + r) % 16
        remote(a2.at[other], a2.at[other], ps.at[0, 0, 0], pr.at[other], sibling).wait_recv()
        return carry

    lax.fori_loop(1, 16, arrival, 0)
    total = a2[0].astype(F32)
    for s in range(1, 16):
        total = total + a2[s].astype(F32)
    total = total * factor
    first_half, second_half = total[:, :64], pltpu.roll(total, 64, 1)[:, :64]
    for m, out in enumerate((out_g, out_u, out_d)):
        out[0:48] = first_half[48 * m : 48 * m + 48].astype(BF16)
        out[48:96] = second_half[48 * m : 48 * m + 48].astype(BF16)

    for copy in sib + [dx_copy, gate_copy]:
        copy.wait_send()
    for t in range(TICKS):
        for way in range(2):
            for step in range(1, 5):
                ring(t, way, step).wait_send()
    for j in range(4):
        for yy in range(2):
            for kk in range(2):
                if (j, yy, kk) == (0, 0, 0):

                    @pl.when(away)
                    def _():
                        deliver_copy(0, 0, 0).wait_send()

                else:
                    deliver_copy(j, yy, kk).wait_send()

    @pl.when(home)
    def _():
        for copy in ring_a() + ring_b() + ring_f(1) + ring_f(2):
            copy.wait_send()
        for t in range(TICKS):
            for copy in up_down(t):
                copy.wait_send()


def per_device(tokens, cotangent, slot_token, slot_gate, w_gate, w_up, w_down):
    factor = float(65536) ** (-0.5)
    vmem = pl.BlockSpec(memory_space=pltpu.VMEM)
    hbm = pl.BlockSpec(memory_space=pl.ANY)
    dma = pltpu.SemaphoreType.DMA
    outs = pl.pallas_call(
        lambda *refs: kernel(factor, *refs),
        out_shape=(
            jax.ShapeDtypeStruct((256, 2048), BF16),
            jax.ShapeDtypeStruct((1, 224), F32),
            jax.ShapeDtypeStruct((96, 64), BF16),
            jax.ShapeDtypeStruct((96, 64), BF16),
            jax.ShapeDtypeStruct((96, 64), BF16),
        ),
        in_specs=[hbm, hbm, vmem, vmem, hbm, hbm, hbm],
        out_specs=(vmem,) * 5,
        scratch_shapes=[
            pltpu.VMEM((512, 2048), BF16),
            pltpu.VMEM((512, 2048), BF16),
            pltpu.VMEM((2, 8, 256), F32),
            pltpu.VMEM((2, 192, 256), F32),
            pltpu.VMEM((2, 96, 256), F32),
            pltpu.VMEM((768, 2048), BF16),
            pltpu.VMEM((384, 2048), BF16),
            pltpu.VMEM((768, 512), BF16),
            pltpu.VMEM((4, 8, 2, 288, 128), BF16),
            pltpu.VMEM((4, 2, 4, 2, 288, 128), BF16),
            pltpu.VMEM((4, 2, 288, 128), F32),
            pltpu.VMEM((4, 2, 2, 144, 128), BF16),
            pltpu.VMEM((16, 144, 128), BF16),
            pltpu.VMEM((256, 2048), F32),
            pltpu.VMEM((256, 2048), F32),
            pltpu.VMEM((256, 2048), F32),
            pltpu.VMEM((8, 256), F32),
            pltpu.VMEM((8, 256), F32),
            dma((7,)),
            dma((5,)),
            dma((5,)),
            dma((6, 2)),
            dma((8, 2)),
            dma((4, 2, 2)),
            dma((4, 2, 4)),
            dma((4, 2, 4)),
            dma((4, 2, 2)),
            dma((16,)),
        ],
        compiler_params=pltpu.CompilerParams(
            collective_id=0, has_side_effects=True, vmem_limit_bytes=56 << 20
        ),
        name="expert_backward",
    )(tokens, cotangent, slot_token.reshape(1, 224), slot_gate.reshape(1, 224), w_gate, w_up, w_down)
    return (outs[0], outs[1].reshape(224), outs[2], outs[3], outs[4])


def solution(mesh):
    both = P(("dp", "blk"), None)
    flat = P(("dp", "blk"))
    rows = P("blk", None)
    block = P("blk", "dp")
    return jax.shard_map(
        per_device,
        mesh=mesh,
        in_specs=(both, both, flat, flat, rows, rows, rows),
        out_specs=(both, flat, block, block, block),
        check_vma=False,
    )
```

time: 1550 us -> 98.8 us (0.06); the launches traced: 1530 us -> 98.5 us
  waiting for transfers between devices: 1380 us -> 0 us
  Pallas kernels: 0 us -> 90.9 us
  matrix products: 56.8 us -> 0 us
  other arithmetic: 28 us -> 0 us
  starting transfers between devices: 20.4 us -> 0 us
  local copies, waits for them, and re-layouts: 26.1 us -> 6.95 us
    reduce_scatter x1 -> x0, waiting for transfers between devices: 1280 us -> none  [per_device(): lax.psum_scatter(terms, ('dp', 'blk'), scatter_dimension=0, tiled=True)[0]]
    ppermute x21 -> x0, waiting for transfers between devices: 104 us -> none  [passed_along(): lax.ppermute(shard, axis, [(i, (i + by) % size) for i in range(size)])]
    pallas_call x0 -> x1, Pallas kernels: none -> 90.9 us  [per_device(): pl.pallas_call(lambda *refs: kernel(factor, *refs), out_shape=(jax.ShapeD...]
    dot_general x64 -> x0, matrix products: 56.8 us -> none  [the longest x24 24 us: row_dot(): lax.dot_general(left, right, (((1,), (1,)), ((), ())), preferred_element_...]
    ppermute x21 -> x0, starting transfers between devices: 20.3 us -> none  [passed_along(): lax.ppermute(shard, axis, [(i, (i + by) % size) for i in range(size)])]
    dynamic_update_slice x8 -> x0, other arithmetic: 18.3 us -> none  [per_device(): lax.dynamic_update_slice_in_dim(partial_value, block[:, None], owner, 1)]
  transfers between devices with their start and end apart: 22 -> 0, of which waited for: 17 -> 0; matrix products, arithmetic and copies ran while one was open for 5% -> 0% of each run, Pallas kernels for 0% -> 0%
where the time goes in v1:
time: 98.8 us; the launch traced here: 98.5 us
  Pallas kernels  90.9 us (92%)
  local copies, waits for them, and re-layouts  6.95 us (7%)
    pallas_call x1, Pallas kernels, per_device(): pl.pallas_call(lambda *refs: kernel(factor, *refs), out_shape=(jax.ShapeD...  90.9 us
    unnamed x13, local copies, waits for them, and re-layouts  6.39 us

profile of v1, /device:TPU:1, one launch (start us, length us, event | category | flops | bytes accessed | tf_op | source)
XLA Modules:
  0.0 98.5 jit_solution(17017517437949309667)
XLA Ops:
  0.6 0.0 copy-start.3
  0.6 0.6 copy-done.3
  1.3 0.6 reshape.20.refs_3_
  1.9 90.9 %expert_backward.1 = (bf16[256,2048]{1,0:T(8,128)(2,1)}, f32[1,224]{1,0:T(1,128)}, bf16[96,64]{1,0:T(8,128)(2,1)}, bf16[96,64]{1,0:T(8,128)(2,1)}, bf16[96,64]{1,0:T(8,128)(2,1)}) custom-call(bf16[256,2048]{1,0:T(8,128)(2,1)} %refs_0_.1, bf16[256,2048]{1,0:T(8,128)(2,1)} %refs_1_.1, s32[1,224]{1,0:T(1,128)} %bitcast.2, bf16[1,224]{1,0:T(2,128)(2,1)} %reshape.20.refs_3_, ...), custom_call_target="tpu_custom_call" | custom-call | tf_op jit(solution)/shard_map/expert_backward/pallas_call | solution.py:407
  92.7 0.0 copy-start.1
  92.7 1.4 %copy.12 = bf16[96,64]{0,1:T(8,128)(2,1)} copy(bf16[96,64]{1,0:T(8,128)(2,1)} %get-tuple-element.17) | data formatting | bytes 24576
  94.2 0.0 copy-done.1
  94.2 0.0 copy-start
  94.2 0.7 copy.13
  94.9 0.0 copy-done
  94.9 0.7 copy.14
  95.6 0.0 copy-start.2
  95.6 2.3 %copy.17 = bf16[256,2048]{1,0:T(8,128)(2,1)} copy(bf16[256,2048]{1,0:T(8,128)(2,1)} %get-tuple-element.25) | data formatting | bytes 2097152
  97.9 0.0 copy-done.2
  97.9 0.6 copy.18
Async XLA Ops:
  0.6 0.7 copy-start.3
  92.7 1.4 %copy-start.1 = (bf16[96,64]{1,0:T(8,128)(2,1)S(1)}, bf16[96,64]{1,0:T(8,128)(2,1)}, u32[]{:S(2)}) copy-start(bf16[96,64]{1,0:T(8,128)(2,1)} %get-tuple-element.18) | copy-start | bytes 36868
  94.2 0.7 copy-start
  95.6 2.3 %copy-start.2 = (f32[1,224]{1,0:T(1,128)S(1)}, f32[1,224]{1,0:T(1,128)}, u32[]{:S(2)}) copy-start(f32[1,224]{1,0:T(1,128)} %get-tuple-element.11) | copy-start | bytes 2692

commit v2 on v1

v2 whole, which is shorter than its diff:
```python
import jax
import jax.numpy as jnp
from jax import lax
from jax.experimental import pallas as pl
from jax.experimental.pallas import tpu as pltpu
from jax.sharding import PartitionSpec as P

MESH = pl.DeviceIdType.MESH
F32 = jnp.float32
BF16 = jnp.bfloat16
TICKS = 4

RINGS = (
    (0, ((0, 0),)),
    (1, ((0, 1),)),
    (2, ((0, 0),)),
    (3, ((0, 0),)),
    (0, ((1, 1),)),
    (3, ((1, 1),)),
)


def dot_nt(a, b):
    return lax.dot_general(a, b, (((1,), (1,)), ((), ())), preferred_element_type=F32)


def dot_nn(a, b):
    return lax.dot_general(a, b, (((1,), (0,)), ((), ())), preferred_element_type=F32)


def kernel(
    factor, tok, cot, slot, gate, wg, wu, wd,
    out_x, out_gate, out_g, out_u, out_d,
    xb, db, xt, dt, cb, ups, raws, wgu, wdn, dgs, qs, grad, recv, fin, side, pack, a2, acc, dxo, dxs, dxr, gs, gr,
    loc_sem, sib_s, sib_r, ax_s, ay_s, ag_r, zs, zr, xs_, xr, ps, pr,
):
    dp, blk = lax.axis_index("dp"), lax.axis_index("blk")
    c, z, yh = dp % 2, (dp // 2) % 8, dp // 16
    x, yl = blk % 4, blk // 4
    y = yh * 2 + yl
    home = c == yl
    away = c != yl

    def device(xx, yy, zz, cc):
        return ((yy // 2) * 16 + zz * 2 + cc, (yy % 2) * 4 + xx)

    right, left = device((x + 1) % 4, y, z, c), device((x + 3) % 4, y, z, c)
    above, below = device(x, (y + 1) % 4, z, c), device(x, (y + 3) % 4, z, c)
    zside = (device(x, y, (z + 1) % 8, c), device(x, y, (z + 7) % 8, c))
    sibling = device(x, y, z, 1 - c)
    place = y * 4 + x

    loads = [
        pltpu.make_async_copy(tok, xb.at[pl.ds(0, 256)], loc_sem.at[0]),
        pltpu.make_async_copy(cot, db.at[pl.ds(0, 256)], loc_sem.at[1]),
    ]
    wloads = [
        pltpu.make_async_copy(wg.at[pl.ds(0, 48)], wgu.at[pl.ds(0, 48)], loc_sem.at[2]),
        pltpu.make_async_copy(wu.at[pl.ds(0, 48)], wgu.at[pl.ds(48, 48)], loc_sem.at[3]),
        pltpu.make_async_copy(wg.at[pl.ds(48, 48)], wgu.at[pl.ds(96, 48)], loc_sem.at[4]),
        pltpu.make_async_copy(wu.at[pl.ds(48, 48)], wgu.at[pl.ds(144, 48)], loc_sem.at[5]),
        pltpu.make_async_copy(wd, wdn.at[pl.ds(0, 96)], loc_sem.at[6]),
    ]

    @pl.when(home)
    def _():
        for copy in wloads:
            copy.start()

    for copy in loads:
        copy.start()

    barrier = pltpu.get_barrier_semaphore()

    def greet(target):
        pl.semaphore_signal(barrier, inc=1, device_id=target, device_id_type=MESH)

    greet(zside[0])
    greet(zside[1])
    greet(sibling)

    def greet_plane(r, carry):
        other = (place + r) % 16
        greet(device(other % 4, other // 4, z, yl))
        return carry

    lax.fori_loop(1, 16, greet_plane, 0)

    @pl.when(away)
    def _():
        greet(above)
        greet(below)
        greet(right)
        greet(left)

    slots = jnp.broadcast_to(slot[...].astype(F32), (128, 224)).T[:, 0:1]
    gates = jnp.broadcast_to(gate[...].astype(F32).reshape(1, 224), (128, 224)).T[:, 0:1]
    token_of = lax.broadcasted_iota(jnp.int32, (224, 256), 1).astype(F32)
    named = token_of == slots
    cb[0] = jnp.broadcast_to(
        jnp.sum(jnp.where(named, gates, 0.0), axis=0, keepdims=True), (8, 256)
    )

    @pl.when(home)
    def _():
        for copy in wloads:
            copy.wait()

    for copy in loads:
        copy.wait()
    pl.semaphore_wait(barrier, jnp.where(home, 19, 21))

    def remote(src, dst, s_sem, r_sem, target):
        return pltpu.make_async_remote_copy(
            src_ref=src, dst_ref=dst, send_sem=s_sem, recv_sem=r_sem,
            device_id=target, device_id_type=MESH,
        )

    def unit(t, i):
        return (wgu.at[pl.ds(192 * t + 96 * i, 96)], wdn.at[pl.ds(96 * t + 48 * i, 48)])

    def send_unit(src, dst, sem, n, target):
        a, b = unit(*src), unit(*dst)
        return [
            remote(a[p], b[p], sem.at[n, p], ag_r.at[dst[0], dst[1], p], target)
            for p in range(2)
        ]

    def ring_a():
        return send_unit((0, 0), (1, 0), ax_s, 0, right) + send_unit((0, 1), (1, 1), ax_s, 1, left)

    def ring_b():
        return send_unit((0, 1), (2, 0), ax_s, 2, right) + send_unit((0, 0), (2, 1), ax_s, 3, left)

    def ring_f():
        return send_unit((1, 0), (3, 0), ax_s, 4, right) + send_unit((1, 1), (3, 1), ax_s, 5, left)

    def up_down(t):
        copies = send_unit((t, 0), (t, 0), ay_s, 2 * t, below) + send_unit((t, 1), (t, 1), ay_s, 2 * t + 1, above)
        return copies if t < 3 else copies[1::2]

    def away_f():
        return ring_f()[0::2]

    def start(copies):
        for copy in copies:
            copy.start()

    def wait_unit(t, i):
        for p in range(2):
            ref = unit(t, i)[p]
            remote(ref, ref, ax_s.at[0, p], ag_r.at[t, i, p], sibling).wait_recv()

    sib = [
        remote(xb.at[pl.ds(0, 256)], xb.at[pl.ds(256, 256)], sib_s.at[0], sib_r.at[0], sibling),
        remote(db.at[pl.ds(0, 256)], db.at[pl.ds(256, 256)], sib_s.at[1], sib_r.at[1], sibling),
        remote(cb.at[0], cb.at[1], sib_s.at[2], sib_r.at[2], sibling),
    ]

    @pl.when(home)
    def _():
        start(ring_a() + up_down(0))

    start(sib)

    gate_acc = [jnp.zeros((1, 512), F32)]

    def forward_part(t):
        top, low = 192 * t, 96 * t

        ups[...] = dot_nn(wgu[pl.ds(top, 192)], xt[...])
        raws[...] = dot_nn(wdn[pl.ds(low, 96)], dt[...])
        gu = ups[...]
        raw2 = raws[...]
        weight = jnp.concatenate([cb[0, 0:1], cb[1, 0:1]], axis=1)
        scaled = []
        for i in range(2):
            g = gu[96 * i : 96 * i + 48]
            u = gu[96 * i + 48 : 96 * i + 96]
            raw = raw2[48 * i : 48 * i + 48]
            sig = 1.0 / (1.0 + jnp.exp(-g))
            act = g * sig
            hid = act * u
            stored = hid.astype(BF16).astype(F32)
            gate_acc[0] = gate_acc[0] + jnp.sum(stored * raw, axis=0, keepdims=True)
            dh = weight * raw
            dgs[pl.ds(top + 96 * i, 48)] = (dh * u * sig * (1.0 + g * (1.0 - sig))).astype(BF16)
            dgs[pl.ds(top + 96 * i + 48, 48)] = (dh * act).astype(BF16)
            scaled.append((weight * hid).astype(BF16))
        qs[...] = jnp.concatenate(scaled, axis=0)

    def grad_part(t):
        q = qs[...]
        dgu = dgs[pl.ds(192 * t, 192)]

        for n in range(8):
            cols = slice(256 * n, 256 * n + 256)
            part = dot_nn(dgu, xb[:, cols]).astype(BF16)
            for k in range(2):
                lanes = slice(128 * k, 128 * k + 128)
                place_at = grad.at[t, 2 * (n % 4) + k, n // 4]
                place_at[0:96] = part[0:96, lanes]
                place_at[144:240] = part[96:192, lanes]
        for n in range(8):
            cols = slice(256 * n, 256 * n + 256)
            down = dot_nn(q, db[:, cols]).astype(BF16)
            for k in range(2):
                lanes = slice(128 * k, 128 * k + 128)
                place_at = grad.at[t, 2 * (n % 4) + k, n // 4]
                place_at[96:144] = down[0:48, lanes]
                place_at[240:288] = down[48:96, lanes]

    def sends(ring, way, step):
        t, parts = ring
        return tuple(h for h, far in parts if step > 1 or far == way)

    def ring_copy(r, way, step):
        t = RINGS[r][0]
        half = sends(RINGS[r], way, step)
        sign = 1 if way == 0 else 7
        dest = (z + sign * (5 - step)) % 8
        if len(half) == 2:
            src, dst = grad.at[t, dest], recv.at[t, way, step - 1]
        else:
            src, dst = grad.at[t, dest, half[0]], recv.at[t, way, step - 1, half[0]]
        return remote(src, dst, zs.at[r, way, step - 1], zr.at[r, way, step - 1], zside[way])

    def stage_step(r, way, stage):
        return stage if sends(RINGS[r], way, 1) else stage + 1

    def first(r):
        for way in range(2):
            ring_copy(r, way, stage_step(r, way, 1)).start()

    def pass_on(r, stage):
        t = RINGS[r][0]
        for way in range(2):
            step = stage_step(r, way, stage)
            if step > 4:
                continue
            ring_copy(r, way, step - 1).wait_recv()
            sign = 1 if way == 0 else 7
            dest = (z + sign * (5 - step)) % 8
            for h in sends(RINGS[r], way, step - 1):
                total = grad[t, dest, h].astype(F32) + recv[t, way, step - 2, h].astype(F32)
                grad[t, dest, h] = total.astype(BF16)
            ring_copy(r, way, step).start()

    def finish(r):
        t, parts = RINGS[r]
        for way in range(2):
            ring_copy(r, way, 4).wait_recv()
        for h, _ in parts:
            fin[t, h] = (
                grad[t, z, h].astype(F32) + recv[t, 0, 3, h].astype(F32) + recv[t, 1, 3, h].astype(F32)
            )

    def side_copy(t, i):
        return remote(
            grad.at[t, :, 1, pl.ds(144 * i, 144)], side.at[t - 1, i],
            xs_.at[t - 1, i], xr.at[t - 1, i], left if i == 0 else right,
        )

    def side_send(t):
        for i in range(2):
            side_copy(t, i).start()

    def side_merge():
        for t in (1, 2):
            for i in range(2):
                side_copy(t, i).wait_recv()
        for i in range(2):
            rows = pl.ds(144 * i, 144)
            for k in range(8):
                total = grad[0, k, 1, rows].astype(F32) + side[0, i, k].astype(F32) + side[1, 1 - i, k].astype(F32)
                grad[0, k, 1, rows] = total.astype(BF16)

    low_lanes = lax.broadcasted_iota(jnp.int32, (144, 128), 1) < 64
    halves = (((0, 0), (0, 1)), ((1, 0), (2, 0)), ((2, 1), (1, 1)), ((3, 0), (3, 1)))
    offset = (0, 3, 1, 2)

    def rows_of(t, i, h):
        return fin[t, h, pl.ds(144 * i, 144)]

    def deliver_copy(j, h, kk):
        k = (c + kk) % 2
        target = device((x + offset[j]) % 4, 2 * h + c, z, k)
        return remote(pack.at[j, h, k], a2.at[place], ps.at[j, h, kk], pr.at[place], target)

    def deliver(j, h):
        a, b = rows_of(*halves[j][0], h), rows_of(*halves[j][1], h)
        pack[j, h, 0] = jnp.where(low_lanes, a, pltpu.roll(b, 64, 1)).astype(BF16)
        pack[j, h, 1] = jnp.where(low_lanes, pltpu.roll(a, 64, 1), b).astype(BF16)
        for kk in range(2):
            if (j, kk) == (0, 0):
                mine = jnp.logical_and(home, yh == h)

                @pl.when(mine)
                def _():
                    a2[place] = pack[0, h, c]

                @pl.when(jnp.logical_not(mine))
                def _():
                    deliver_copy(0, h, 0).start()

            else:
                deliver_copy(j, h, kk).start()

    dx_copy = remote(dxs, dxr, sib_s.at[3], sib_r.at[3], sibling)
    gate_copy = remote(gs, gr, sib_s.at[4], sib_r.at[4], sibling)

    def token_part():
        gs[...] = jnp.broadcast_to(gate_acc[0][:, 256:], (8, 256))
        gate_copy.start()
        left_side = dgs[...].T

        for n in range(8):
            cols = slice(256 * n, 256 * n + 256)
            part = dot_nn(left_side, wgu[:, cols])
            dxo[:, cols] = part[:256]
            dxs[:, cols] = part[256:]
        dx_copy.start()

    def weights_of(t):
        @pl.when(away)
        def _():
            wait_unit(t, 0)
            wait_unit(t, 1)
            if t == 1:
                start(away_f())

        if t > 0:

            @pl.when(home)
            def _():
                wait_unit(t, 0)
                wait_unit(t, 1)
                start((ring_f() if t == 1 else []) + up_down(t))

    xt[:, 0:256] = xb[0:256].T
    dt[:, 0:256] = db[0:256].T
    for copy in sib:
        copy.wait_recv()
    xt[:, 256:512] = xb[256:512].T
    dt[:, 256:512] = db[256:512].T
    weights_of(0)
    forward_part(0)

    @pl.when(home)
    def _():
        start(ring_b())

    grad_part(0)
    first(0)
    pass_on(0, 2)
    weights_of(1)
    forward_part(1)
    grad_part(1)
    first(1)

    @pl.when(away)
    def _():
        side_send(1)

    pass_on(0, 3)
    pass_on(1, 2)
    pass_on(0, 4)
    weights_of(2)
    forward_part(2)
    grad_part(2)
    first(2)

    @pl.when(away)
    def _():
        side_send(2)

    finish(0)
    deliver(0, 0)
    pass_on(1, 3)
    pass_on(2, 2)
    pass_on(1, 4)
    weights_of(3)
    forward_part(3)
    grad_part(3)
    first(3)
    first(5)

    @pl.when(home)
    def _():
        side_send(1)
        side_send(2)

    pass_on(2, 3)
    finish(1)
    token_part()
    pass_on(2, 4)
    pass_on(3, 2)
    pass_on(5, 2)
    side_merge()
    first(4)
    finish(2)
    deliver(1, 0)
    deliver(2, 0)
    pass_on(3, 3)
    pass_on(5, 3)
    pass_on(4, 2)
    pass_on(3, 4)
    pass_on(5, 4)
    pass_on(4, 3)
    gate_copy.wait_recv()
    gate_tok = gate_acc[0][:, :256] + gr[0:1]
    column = jnp.sum(jnp.where(named, gate_tok, 0.0), axis=1, keepdims=True)
    out_gate[...] = jnp.broadcast_to(column, (224, 128)).T[0:1]
    dx_copy.wait_recv()
    out_x[...] = (dxo[...] + dxr[...]).astype(BF16)

    finish(3)
    deliver(3, 0)
    finish(5)
    deliver(3, 1)
    pass_on(4, 4)
    finish(4)
    deliver(0, 1)

    def source(r):
        return ((y + r // 4) % 4) * 4 + (x + r % 4) % 4

    def arrive(other):
        remote(a2.at[other], a2.at[other], ps.at[0, 0, 0], pr.at[other], sibling).wait_recv()

    @pl.when(away)
    def _():
        arrive(place)

    for r in (4, 8, 12, 2, 6, 10, 14):
        arrive(source(r))

    total = a2[place].astype(F32)
    for r in (4, 8, 12, 2, 6, 10, 14):
        total = total + a2[source(r)].astype(F32)
    acc[...] = total

    @pl.when(yh == 0)
    def _():
        extra = acc[...]
        for r in (1, 5, 9, 13, 3, 7, 11, 15):
            arrive(source(r))
            extra = extra + a2[source(r)].astype(F32)
        acc[...] = extra

    for m, out in enumerate((out_g, out_u, out_d)):
        block = (acc[48 * m : 48 * m + 48] * factor).T
        out[...] = jnp.concatenate([block[:64], block[64:]], axis=1).astype(BF16)

    for copy in sib + [dx_copy, gate_copy]:
        copy.wait_send()
    for r in range(6):
        for way in range(2):
            for step in range(1, 5):
                if sends(RINGS[r], way, step):
                    ring_copy(r, way, step).wait_send()
    for t in (1, 2):
        for i in range(2):
            side_copy(t, i).wait_send()
    for j, h in ((0, 0), (1, 0), (2, 0), (3, 0), (0, 1), (3, 1)):
        for kk in range(2):
            if (j, kk) == (0, 0):

                @pl.when(jnp.logical_not(jnp.logical_and(home, yh == h)))
                def _():
                    deliver_copy(0, h, 0).wait_send()

            else:
                deliver_copy(j, h, kk).wait_send()

    @pl.when(away)
    def _():
        for copy in away_f():
            copy.wait_send()

    @pl.when(home)
    def _():
        for copy in ring_a() + ring_b() + ring_f():
            copy.wait_send()
        for t in range(TICKS):
            for copy in up_down(t):
                copy.wait_send()


def hand_over(*refs):
    copies = [
        pltpu.make_async_copy(refs[i], refs[5 + i], refs[10].at[i]) for i in range(5)
    ]
    for copy in copies:
        copy.start()
    for copy in copies:
        copy.wait()


def per_device(tokens, cotangent, slot_token, slot_gate, w_gate, w_up, w_down):
    factor = float(65536) ** (-0.5)
    vmem = pl.BlockSpec(memory_space=pltpu.VMEM)
    hbm = pl.BlockSpec(memory_space=pl.ANY)
    dma = pltpu.SemaphoreType.DMA
    outs = pl.pallas_call(
        lambda *refs: kernel(factor, *refs),
        out_shape=(
            jax.ShapeDtypeStruct((256, 2048), BF16),
            jax.ShapeDtypeStruct((1, 224), F32),
            jax.ShapeDtypeStruct((64, 96), BF16),
            jax.ShapeDtypeStruct((64, 96), BF16),
            jax.ShapeDtypeStruct((64, 96), BF16),
        ),
        in_specs=[hbm, hbm, vmem, vmem, hbm, hbm, hbm],
        out_specs=(vmem,) * 5,
        scratch_shapes=[
            pltpu.VMEM((512, 2048), BF16),
            pltpu.VMEM((512, 2048), BF16),
            pltpu.VMEM((2048, 512), BF16),
            pltpu.VMEM((2048, 512), BF16),
            pltpu.VMEM((2, 8, 256), F32),
            pltpu.VMEM((192, 512), F32),
            pltpu.VMEM((96, 512), F32),
            pltpu.VMEM((768, 2048), BF16),
            pltpu.VMEM((384, 2048), BF16),
            pltpu.VMEM((768, 512), BF16),
            pltpu.VMEM((96, 512), BF16),
            pltpu.VMEM((4, 8, 2, 288, 128), BF16),
            pltpu.VMEM((4, 2, 4, 2, 288, 128), BF16),
            pltpu.VMEM((4, 2, 288, 128), F32),
            pltpu.VMEM((2, 2, 8, 144, 128), BF16),
            pltpu.VMEM((4, 2, 2, 144, 128), BF16),
            pltpu.VMEM((16, 144, 128), BF16),
            pltpu.VMEM((144, 128), F32),
            pltpu.VMEM((256, 2048), F32),
            pltpu.VMEM((256, 2048), F32),
            pltpu.VMEM((256, 2048), F32),
            pltpu.VMEM((8, 256), F32),
            pltpu.VMEM((8, 256), F32),
            dma((7,)),
            dma((5,)),
            dma((5,)),
            dma((6, 2)),
            dma((8, 2)),
            dma((4, 2, 2)),
            dma((6, 2, 4)),
            dma((6, 2, 4)),
            dma((2, 2)),
            dma((2, 2)),
            dma((4, 2, 2)),
            dma((16,)),
        ],
        compiler_params=pltpu.CompilerParams(
            collective_id=0, has_side_effects=True, vmem_limit_bytes=56 << 20
        ),
        name="expert_backward",
    )(tokens, cotangent, slot_token.reshape(1, 224), slot_gate, w_gate, w_up, w_down)
    outs = pl.pallas_call(
        hand_over,
        out_shape=[jax.ShapeDtypeStruct(o.shape, o.dtype) for o in outs],
        in_specs=[vmem] * 5,
        out_specs=[hbm] * 5,
        scratch_shapes=[dma((5,))],
        name="hand_over",
    )(*outs)
    return (outs[0], outs[1].reshape(224), outs[2].T, outs[3].T, outs[4].T)


def solution(mesh):
    both = P(("dp", "blk"), None)
    flat = P(("dp", "blk"))
    rows = P("blk", None)
    block = P("blk", "dp")
    return jax.shard_map(
        per_device,
        mesh=mesh,
        in_specs=(both, both, flat, flat, rows, rows, rows),
        out_specs=(both, flat, block, block, block),
        check_vma=False,
    )
```

time: 98.8 us -> 79.4 us (0.80)
  the two profiles are of different devices: /device:TPU:1 before, /device:TPU:17 now
where the time goes in v2:
time: 79.4 us; the launch traced here: 79.3 us
  Pallas kernels  78.6 us (99%)
    pallas_call x1, Pallas kernels, per_device(): pl.pallas_call(lambda *refs: kernel(factor, *refs), out_shape=(jax.ShapeD...  76.4 us
    pallas_call x1, Pallas kernels, per_device(): pl.pallas_call(hand_over, out_shape=[jax.ShapeDtypeStruct(o.shape, o.dtyp...  2.27 us

profile of v2, /device:TPU:17, one launch (start us, length us, event | category | flops | bytes accessed | tf_op | source)
XLA Modules:
  0.0 79.3 jit_solution(13079140328596828218)
XLA Ops:
  0.6 76.4 %expert_backward.1 = (bf16[256,2048]{1,0:T(8,128)(2,1)}, f32[1,224]{1,0:T(1,128)}, bf16[64,96]{1,0:T(8,128)(2,1)}, bf16[64,96]{1,0:T(8,128)(2,1)}, bf16[64,96]{1,0:T(8,128)(2,1)}) custom-call(bf16[256,2048]{1,0:T(8,128)(2,1)} %refs_0_.1, bf16[256,2048]{1,0:T(8,128)(2,1)} %refs_1_.1, s32[1,224]{1,0:T(1,128)} %bitcast.5, bf16[224]{0:T(256)(128)(2,1)} %refs_3_.1, ...), custom_call_target="tpu_custom_call" | custom-call | tf_op jit(solution)/shard_map/expert_backward/pallas_call | solution.py:505
  77.0 2.3 %hand_over.1 = (bf16[256,2048]{1,0:T(8,128)(2,1)}, f32[1,224]{1,0:T(1,128)}, bf16[64,96]{1,0:T(8,128)(2,1)}, bf16[64,96]{1,0:T(8,128)(2,1)}, bf16[64,96]{1,0:T(8,128)(2,1)}) custom-call(bf16[256,2048]{1,0:T(8,128)(2,1)} %get-tuple-element.15.refs_0_, f32[1,224]{1,0:T(1,128)} %get-tuple-element.16.refs_1_, bf16[64,96]{1,0:T(8,128)(2,1)} %get-tuple-element.17.refs_2_, ...), custom_call_target="tpu_custom_call" | custom-call | tf_op jit(solution)/shard_map/hand_over/pallas_call | solution.py:558

commit v3 on v2

--- a/solution.py
+++ b/solution.py
@@ -10,14 +10,9 @@
 BF16 = jnp.bfloat16
 TICKS = 4
 
-RINGS = (
-    (0, ((0, 0),)),
-    (1, ((0, 1),)),
-    (2, ((0, 0),)),
-    (3, ((0, 0),)),
-    (0, ((1, 1),)),
-    (3, ((1, 1),)),
-)
+RINGS = ((0, 0, 0), (1, 0, 1), (2, 0, 0), (3, 0, 0), (0, 1, 1), (3, 1, 1))
+SHORT = (4,)
+LONG = (3, 5)
 
 
 def dot_nt(a, b):
@@ -31,7 +26,7 @@
 def kernel(
     factor, tok, cot, slot, gate, wg, wu, wd,
     out_x, out_gate, out_g, out_u, out_d,
-    xb, db, xt, dt, cb, ups, raws, wgu, wdn, dgs, qs, grad, recv, fin, side, pack, a2, acc, dxo, dxs, dxr, gs, gr,
+    xb, db, xt, dt, cb, ups, raws, wgu, wdn, dgs, qs, grad, recv, fin, side, pack, a2, acc, ox, dxs, dxr, gs, gr,
     loc_sem, sib_s, sib_r, ax_s, ay_s, ag_r, zs, zr, xs_, xr, ps, pr,
 ):
     dp, blk = lax.axis_index("dp"), lax.axis_index("blk")
@@ -47,6 +42,7 @@
     right, left = device((x + 1) % 4, y, z, c), device((x + 3) % 4, y, z, c)
     above, below = device(x, (y + 1) % 4, z, c), device(x, (y + 3) % 4, z, c)
     zside = (device(x, y, (z + 1) % 8, c), device(x, y, (z + 7) % 8, c))
+    zfar = (device(x, y, (z + 2) % 8, c), device(x, y, (z + 6) % 8, c))
     sibling = device(x, y, z, 1 - c)
     place = y * 4 + x
 
@@ -77,6 +73,8 @@
 
     greet(zside[0])
     greet(zside[1])
+    greet(zfar[0])
+    greet(zfar[1])
     greet(sibling)
 
     def greet_plane(r, carry):
@@ -108,7 +106,7 @@
 
     for copy in loads:
         copy.wait()
-    pl.semaphore_wait(barrier, jnp.where(home, 19, 21))
+    pl.semaphore_wait(barrier, jnp.where(home, 21, 23))
 
     def remote(src, dst, s_sem, r_sem, target):
         return pltpu.make_async_remote_copy(
@@ -210,50 +208,52 @@
                 place_at[96:144] = down[0:48, lanes]
                 place_at[240:288] = down[48:96, lanes]
 
-    def sends(ring, way, step):
-        t, parts = ring
-        return tuple(h for h, far in parts if step > 1 or far == way)
+    def has(r, way, step):
+        return step > 1 or RINGS[r][2] == way
 
     def ring_copy(r, way, step):
-        t = RINGS[r][0]
-        half = sends(RINGS[r], way, step)
-        sign = 1 if way == 0 else 7
-        dest = (z + sign * (5 - step)) % 8
-        if len(half) == 2:
-            src, dst = grad.at[t, dest], recv.at[t, way, step - 1]
-        else:
-            src, dst = grad.at[t, dest, half[0]], recv.at[t, way, step - 1, half[0]]
-        return remote(src, dst, zs.at[r, way, step - 1], zr.at[r, way, step - 1], zside[way])
-
-    def stage_step(r, way, stage):
-        return stage if sends(RINGS[r], way, 1) else stage + 1
+        t, h, _ = RINGS[r]
+        dest = (z + (1, 7)[way] * (5 - step)) % 8
+        target = (zfar if (step == 1 and r not in LONG) or (step == 3 and r in SHORT) else zside)[way]
+        return remote(
+            grad.at[t, dest, h], recv.at[t, way, step - 1, h],
+            zs.at[r, way, step - 1], zr.at[r, way, step - 1], target,
+        )
 
     def first(r):
         for way in range(2):
-            ring_copy(r, way, stage_step(r, way, 1)).start()
-
-    def pass_on(r, stage):
-        t = RINGS[r][0]
+            for step in (1, 2, 4) if r in SHORT else (1, 2):
+                if has(r, way, step) and not (step == 2 and r in LONG and has(r, way, 1)):
+                    ring_copy(r, way, step).start()
+
+    def pass_on(r, step):
+        t, h, _ = RINGS[r]
+        if step == 4 and r in SHORT:
+            return
+        if step == 2 and r not in LONG:
+            return
         for way in range(2):
-            step = stage_step(r, way, stage)
-            if step > 4:
+            if step == 2 and not has(r, way, 1):
                 continue
+            dest = (z + (1, 7)[way] * (5 - step)) % 8
             ring_copy(r, way, step - 1).wait_recv()
-            sign = 1 if way == 0 else 7
-            dest = (z + sign * (5 - step)) % 8
-            for h in sends(RINGS[r], way, step - 1):
-                total = grad[t, dest, h].astype(F32) + recv[t, way, step - 2, h].astype(F32)
-                grad[t, dest, h] = total.astype(BF16)
+            total = grad[t, dest, h].astype(F32) + recv[t, way, step - 2, h].astype(F32)
+            if step == 3 and has(r, way, 1) and r not in LONG:
+                ring_copy(r, way, 1).wait_recv()
+                total = total + recv[t, way, 0, h].astype(F32)
+            grad[t, dest, h] = total.astype(BF16)
             ring_copy(r, way, step).start()
 
     def finish(r):
-        t, parts = RINGS[r]
+        t, h, _ = RINGS[r]
         for way in range(2):
             ring_copy(r, way, 4).wait_recv()
-        for h, _ in parts:
-            fin[t, h] = (
-                grad[t, z, h].astype(F32) + recv[t, 0, 3, h].astype(F32) + recv[t, 1, 3, h].astype(F32)
-            )
+        total = grad[t, z, h].astype(F32) + recv[t, 0, 3, h].astype(F32) + recv[t, 1, 3, h].astype(F32)
+        if r in SHORT:
+            for way in range(2):
+                ring_copy(r, way, 3).wait_recv()
+            total = total + recv[t, 0, 2, h].astype(F32) + recv[t, 1, 2, h].astype(F32)
+        fin[t, h] = total
 
     def side_copy(t, i):
         return remote(
@@ -309,33 +309,31 @@
     dx_copy = remote(dxs, dxr, sib_s.at[3], sib_r.at[3], sibling)
     gate_copy = remote(gs, gr, sib_s.at[4], sib_r.at[4], sibling)
 
-    def token_part():
-        gs[...] = jnp.broadcast_to(gate_acc[0][:, 256:], (8, 256))
-        gate_copy.start()
-        left_side = dgs[...].T
-
+    def sibling_rows(k):
+        left_side = dgs[pl.ds(384 * k, 384), 256:512].T
         for n in range(8):
             cols = slice(256 * n, 256 * n + 256)
-            part = dot_nn(left_side, wgu[:, cols])
-            dxo[:, cols] = part[:256]
-            dxs[:, cols] = part[256:]
-        dx_copy.start()
-
-    def weights_of(t):
-        @pl.when(away)
-        def _():
-            wait_unit(t, 0)
-            wait_unit(t, 1)
+            part = dot_nn(left_side, wgu[pl.ds(384 * k, 384), cols])
+            dxs[:, cols] = part if k == 0 else dxs[:, cols] + part
+
+    def own_rows():
+        left_side = dgs[:, 0:256].T
+        for n in range(8):
+            cols = slice(256 * n, 256 * n + 256)
+            ox[:, cols] = (dot_nn(left_side, wgu[:, cols]) + dxr[:, cols]).astype(BF16)
+
+    def away_weights(t):
+        wait_unit(t, 0)
+        wait_unit(t, 1)
+        if t == 1:
+            start(away_f())
+
+    def home_weights(t):
+        for i in range(2):
+            wait_unit(t, i)
             if t == 1:
-                start(away_f())
-
-        if t > 0:
-
-            @pl.when(home)
-            def _():
-                wait_unit(t, 0)
-                wait_unit(t, 1)
-                start((ring_f() if t == 1 else []) + up_down(t))
+                start(ring_f()[2 * i : 2 * i + 2])
+            start(send_unit((t, i), (t, i), ay_s, 2 * t + i, (below, above)[i])[1 if t == 3 else 0 :])
 
     xt[:, 0:256] = xb[0:256].T
     dt[:, 0:256] = db[0:256].T
@@ -343,7 +341,11 @@
         copy.wait_recv()
     xt[:, 256:512] = xb[256:512].T
     dt[:, 256:512] = db[256:512].T
-    weights_of(0)
+
+    @pl.when(away)
+    def _():
+        away_weights(0)
+
     forward_part(0)
 
     @pl.when(home)
@@ -352,34 +354,63 @@
 
     grad_part(0)
     first(0)
-    pass_on(0, 2)
-    weights_of(1)
+
+    @pl.when(home)
+    def _():
+        home_weights(1)
+
+    @pl.when(away)
+    def _():
+        pass_on(0, 2)
+        pass_on(0, 3)
+        away_weights(1)
+
     forward_part(1)
     grad_part(1)
     first(1)
 
+    @pl.when(home)
+    def _():
+        pass_on(0, 2)
+        pass_on(0, 3)
+        home_weights(2)
+        pass_on(1, 2)
+        pass_on(0, 4)
+        pass_on(1, 3)
+
     @pl.when(away)
     def _():
         side_send(1)
-
-    pass_on(0, 3)
-    pass_on(1, 2)
-    pass_on(0, 4)
-    weights_of(2)
+        pass_on(0, 4)
+        pass_on(1, 2)
+        pass_on(1, 3)
+
+    sibling_rows(0)
+
+    @pl.when(away)
+    def _():
+        away_weights(2)
+
     forward_part(2)
     grad_part(2)
     first(2)
 
+    @pl.when(home)
+    def _():
+        side_send(1)
+        pass_on(1, 4)
+        home_weights(3)
+        finish(0)
+        deliver(0, 0)
+        pass_on(2, 2)
+        pass_on(2, 3)
+
     @pl.when(away)
     def _():
         side_send(2)
-
-    finish(0)
-    deliver(0, 0)
-    pass_on(1, 3)
-    pass_on(2, 2)
-    pass_on(1, 4)
-    weights_of(3)
+        pass_on(1, 4)
+        away_weights(3)
+
     forward_part(3)
     grad_part(3)
     first(3)
@@ -387,33 +418,38 @@
 
     @pl.when(home)
     def _():
-        side_send(1)
         side_send(2)
-
-    pass_on(2, 3)
+        pass_on(2, 4)
+
+    @pl.when(away)
+    def _():
+        pass_on(2, 2)
+        finish(0)
+        deliver(0, 0)
+        pass_on(2, 3)
+
+    gs[...] = jnp.broadcast_to(gate_acc[0][:, 256:], (8, 256))
+    gate_copy.start()
     finish(1)
-    token_part()
-    pass_on(2, 4)
+    sibling_rows(1)
+    dx_copy.start()
     pass_on(3, 2)
     pass_on(5, 2)
+
+    @pl.when(away)
+    def _():
+        pass_on(2, 4)
+
+    pass_on(3, 3)
+    pass_on(5, 3)
     side_merge()
     first(4)
+    pass_on(3, 4)
+    pass_on(5, 4)
     finish(2)
     deliver(1, 0)
     deliver(2, 0)
-    pass_on(3, 3)
-    pass_on(5, 3)
-    pass_on(4, 2)
-    pass_on(3, 4)
-    pass_on(5, 4)
     pass_on(4, 3)
-    gate_copy.wait_recv()
-    gate_tok = gate_acc[0][:, :256] + gr[0:1]
-    column = jnp.sum(jnp.where(named, gate_tok, 0.0), axis=1, keepdims=True)
-    out_gate[...] = jnp.broadcast_to(column, (224, 128)).T[0:1]
-    dx_copy.wait_recv()
-    out_x[...] = (dxo[...] + dxr[...]).astype(BF16)
-
     finish(3)
     deliver(3, 0)
     finish(5)
@@ -421,6 +457,37 @@
     pass_on(4, 4)
     finish(4)
     deliver(0, 1)
+    gate_copy.wait_recv()
+    gate_tok = gate_acc[0][:, :256] + gr[0:1]
+    column = jnp.sum(jnp.where(named, gate_tok, 0.0), axis=1, keepdims=True)
+    out_gate[...] = jnp.broadcast_to(column, (224, 128)).T[0:1]
+    dx_copy.wait_recv()
+    own_rows()
+    out_copy = pltpu.make_async_copy(ox, out_x, loc_sem.at[7])
+    out_copy.start()
+    for copy in sib + [dx_copy, gate_copy]:
+        copy.wait_send()
+    for r in range(6):
+        for way in range(2):
+            for step in range(1, 5):
+                if has(r, way, step):
+                    ring_copy(r, way, step).wait_send()
+    for t in (1, 2):
+        for i in range(2):
+            side_copy(t, i).wait_send()
+    @pl.when(away)
+    def _():
+        for copy in away_f():
+            copy.wait_send()
+
+    @pl.when(home)
+    def _():
+        for copy in ring_a() + ring_b() + ring_f():
+            copy.wait_send()
+        for t in range(TICKS):
+            for copy in up_down(t):
+                copy.wait_send()
+
 
     def source(r):
         return ((y + r // 4) % 4) * 4 + (x + r % 4) % 4
@@ -452,16 +519,6 @@
         block = (acc[48 * m : 48 * m + 48] * factor).T
         out[...] = jnp.concatenate([block[:64], block[64:]], axis=1).astype(BF16)
 
-    for copy in sib + [dx_copy, gate_copy]:
-        copy.wait_send()
-    for r in range(6):
-        for way in range(2):
-            for step in range(1, 5):
-                if sends(RINGS[r], way, step):
-                    ring_copy(r, way, step).wait_send()
-    for t in (1, 2):
-        for i in range(2):
-            side_copy(t, i).wait_send()
     for j, h in ((0, 0), (1, 0), (2, 0), (3, 0), (0, 1), (3, 1)):
         for kk in range(2):
             if (j, kk) == (0, 0):
@@ -472,28 +529,25 @@
 
             else:
                 deliver_copy(j, h, kk).wait_send()
-
-    @pl.when(away)
-    def _():
-        for copy in away_f():
-            copy.wait_send()
-
-    @pl.when(home)
-    def _():
-        for copy in ring_a() + ring_b() + ring_f():
-            copy.wait_send()
-        for t in range(TICKS):
-            for copy in up_down(t):
-                copy.wait_send()
+    out_copy.wait()
 
 
 def hand_over(*refs):
-    copies = [
-        pltpu.make_async_copy(refs[i], refs[5 + i], refs[10].at[i]) for i in range(5)
-    ]
-    for copy in copies:
+    ins, outs, held = refs[0:5], refs[5:10], refs[10:15]
+    in_sem, out_sem = refs[15], refs[16]
+
+    def pieces(src, dst):
+        whole = [(src[0].at[pl.ds(64 * i, 64)], dst[0].at[pl.ds(64 * i, 64)]) for i in range(4)]
+        return whole + list(zip(src[1:], dst[1:]))
+
+    loads = [pltpu.make_async_copy(p, q, in_sem.at[i]) for i, (p, q) in enumerate(pieces(ins, held))]
+    stores = [pltpu.make_async_copy(p, q, out_sem.at[i]) for i, (p, q) in enumerate(pieces(held, outs))]
+    for copy in loads:
         copy.start()
-    for copy in copies:
+    for i in range(8):
+        loads[i].wait()
+        stores[i].start()
+    for copy in stores:
         copy.wait()
 
 
@@ -512,7 +566,7 @@
             jax.ShapeDtypeStruct((64, 96), BF16),
         ),
         in_specs=[hbm, hbm, vmem, vmem, hbm, hbm, hbm],
-        out_specs=(vmem,) * 5,
+        out_specs=(hbm,) + (vmem,) * 4,
         scratch_shapes=[
             pltpu.VMEM((512, 2048), BF16),
             pltpu.VMEM((512, 2048), BF16),
@@ -532,12 +586,12 @@
             pltpu.VMEM((4, 2, 2, 144, 128), BF16),
             pltpu.VMEM((16, 144, 128), BF16),
             pltpu.VMEM((144, 128), F32),
-            pltpu.VMEM((256, 2048), F32),
+            pltpu.VMEM((256, 2048), BF16),
             pltpu.VMEM((256, 2048), F32),
             pltpu.VMEM((256, 2048), F32),
             pltpu.VMEM((8, 256), F32),
             pltpu.VMEM((8, 256), F32),
-            dma((7,)),
+            dma((8,)),
             dma((5,)),
             dma((5,)),
             dma((6, 2)),
@@ -558,9 +612,9 @@
     outs = pl.pallas_call(
         hand_over,
         out_shape=[jax.ShapeDtypeStruct(o.shape, o.dtype) for o in outs],
-        in_specs=[vmem] * 5,
+        in_specs=[hbm] * 5,
         out_specs=[hbm] * 5,
-        scratch_shapes=[dma((5,))],
+        scratch_shapes=[pltpu.VMEM(o.shape, o.dtype) for o in outs] + [dma((8,)), dma((8,))],
         name="hand_over",
     )(*outs)
     return (outs[0], outs[1].reshape(224), outs[2].T, outs[3].T, outs[4].T)

time: 79.4 us -> 75 us (0.945)
  the two profiles are of different devices: /device:TPU:17 before, /device:TPU:1 now
where the time goes in v3:
time: 75 us; the launch traced here: 74.9 us
  Pallas kernels  74.2 us (99%)
    pallas_call x1, Pallas kernels, per_device(): pl.pallas_call(lambda *refs: kernel(factor, *refs), out_shape=(jax.ShapeD...  72.2 us
    pallas_call x1, Pallas kernels, per_device(): pl.pallas_call(hand_over, out_shape=[jax.ShapeDtypeStruct(o.shape, o.dtyp...  2.06 us

profile of v3, /device:TPU:1, one launch (start us, length us, event | category | flops | bytes accessed | tf_op | source)
XLA Modules:
  0.0 74.9 jit_solution(11043959109878847310)
XLA Ops:
  0.6 72.2 %expert_backward.1 = (bf16[256,2048]{1,0:T(8,128)(2,1)}, f32[1,224]{1,0:T(1,128)}, bf16[64,96]{1,0:T(8,128)(2,1)}, bf16[64,96]{1,0:T(8,128)(2,1)}, bf16[64,96]{1,0:T(8,128)(2,1)}) custom-call(bf16[256,2048]{1,0:T(8,128)(2,1)} %refs_0_.1, bf16[256,2048]{1,0:T(8,128)(2,1)} %refs_1_.1, s32[1,224]{1,0:T(1,128)} %bitcast.5, bf16[224]{0:T(256)(128)(2,1)} %refs_3_.1, ...), custom_call_target="tpu_custom_call" | custom-call | tf_op jit(solution)/shard_map/expert_backward/pallas_call | solution.py:559
  72.8 2.1 %hand_over.1 = (bf16[256,2048]{1,0:T(8,128)(2,1)}, f32[1,224]{1,0:T(1,128)}, bf16[64,96]{1,0:T(8,128)(2,1)}, bf16[64,96]{1,0:T(8,128)(2,1)}, bf16[64,96]{1,0:T(8,128)(2,1)}) custom-call(bf16[256,2048]{1,0:T(8,128)(2,1)} %get-tuple-element.15.refs_0_, f32[1,224]{1,0:T(1,128)} %get-tuple-element.16.refs_1_, bf16[64,96]{1,0:T(8,128)(2,1)} %get-tuple-element.17.refs_2_, ...), custom_call_target="tpu_custom_call" | custom-call | tf_op jit(solution)/shard_map/hand_over/pallas_call | solution.py:612

commit v4 on v3

--- a/solution.py
+++ b/solution.py
@@ -374,6 +374,7 @@
         pass_on(0, 2)
         pass_on(0, 3)
         home_weights(2)
+        side_send(1)
         pass_on(1, 2)
         pass_on(0, 4)
         pass_on(1, 3)
@@ -397,9 +398,9 @@
 
     @pl.when(home)
     def _():
-        side_send(1)
         pass_on(1, 4)
         home_weights(3)
+        side_send(2)
         finish(0)
         deliver(0, 0)
         pass_on(2, 2)
@@ -418,7 +419,6 @@
 
     @pl.when(home)
     def _():
-        side_send(2)
         pass_on(2, 4)
 
     @pl.when(away)

time: 75 us -> 75 us (level)
  no operation moved by 1% of the time
where the time goes in v4:
time: 75 us; the launch traced here: 74.9 us
  Pallas kernels  74.2 us (99%)
    pallas_call x1, Pallas kernels, per_device(): pl.pallas_call(lambda *refs: kernel(factor, *refs), out_shape=(jax.ShapeD...  72.2 us
    pallas_call x1, Pallas kernels, per_device(): pl.pallas_call(hand_over, out_shape=[jax.ShapeDtypeStruct(o.shape, o.dtyp...  2.06 us

profile of v4, /device:TPU:1, one launch (start us, length us, event | category | flops | bytes accessed | tf_op | source)
XLA Modules:
  0.0 74.9 jit_solution(348519751364853389)
XLA Ops:
  0.6 72.2 %expert_backward.1 = (bf16[256,2048]{1,0:T(8,128)(2,1)}, f32[1,224]{1,0:T(1,128)}, bf16[64,96]{1,0:T(8,128)(2,1)}, bf16[64,96]{1,0:T(8,128)(2,1)}, bf16[64,96]{1,0:T(8,128)(2,1)}) custom-call(bf16[256,2048]{1,0:T(8,128)(2,1)} %refs_0_.1, bf16[256,2048]{1,0:T(8,128)(2,1)} %refs_1_.1, s32[1,224]{1,0:T(1,128)} %bitcast.5, bf16[224]{0:T(256)(128)(2,1)} %refs_3_.1, ...), custom_call_target="tpu_custom_call" | custom-call | tf_op jit(solution)/shard_map/expert_backward/pallas_call | solution.py:559
  72.8 2.1 %hand_over.1 = (bf16[256,2048]{1,0:T(8,128)(2,1)}, f32[1,224]{1,0:T(1,128)}, bf16[64,96]{1,0:T(8,128)(2,1)}, bf16[64,96]{1,0:T(8,128)(2,1)}, bf16[64,96]{1,0:T(8,128)(2,1)}) custom-call(bf16[256,2048]{1,0:T(8,128)(2,1)} %get-tuple-element.15.refs_0_, f32[1,224]{1,0:T(1,128)} %get-tuple-element.16.refs_1_, bf16[64,96]{1,0:T(8,128)(2,1)} %get-tuple-element.17.refs_2_, ...), custom_call_target="tpu_custom_call" | custom-call | tf_op jit(solution)/shard_map/hand_over/pallas_call | solution.py:612
